TPU v7x, 512 devices: a whole 4x8x8 slice. The times are simulated.
512 devices in a mesh: replica: 64 (over x, y, z_hi), fsdp: 8 (over z_lo, core).
Axes of the slice: x: 4, y: 8, z: 8 (z_hi: 2, z_lo: 4; z = z_hi * 4 + z_lo), core: 2. Of those that a mesh axis runs over, the one named last changes fastest.
Arguments:
- partner: int32 [64], replicated, may hold values from 0 to 63, as said below
- pseudo_grad: bfloat16 [64, 4096, 512], P('replica', 'fsdp'), may hold values from -6 to 6
- momentum: bfloat16 [64, 4096, 512], P('replica', 'fsdp'), may hold values from -4 to 4
- outer_params: bfloat16 [64, 4096, 512], P('replica', 'fsdp'), may hold values from -6 to 6
- activations: bfloat16 [64, 1024, 4096], P('replica', 'fsdp'), may hold values from -6 to 6
- norm_gain: float32 [64, 4096], P('replica'), may hold values from 0.1 to 1.9
- key_weight: bfloat16 [64, 4096, 512], P('replica', 'fsdp'), may hold values from -0.09375 to 0.09375
- key_cotangent: bfloat16 [64, 1024, 512], P('replica', 'fsdp'), may hold values from -6 to 6
Outputs:
- new_params: bfloat16 [64, 4096, 512], P('replica', 'fsdp')
- new_momentum: bfloat16 [64, 4096, 512], P('replica', 'fsdp')
- keys: bfloat16 [64, 1024, 512], P('replica', 'fsdp')
- weight_grad: bfloat16 [64, 4096, 512], P('replica', 'fsdp')
- gain_grad: float32 [64, 4096], P('replica')
Inputs may be any that keep to these rules, and one draw needn't show every extreme that they name: partner[partner[r]] == r and partner[r] != r for every replica r: the replicas form 64 / 2 disjoint pairs.
All inputs are finite; a program needn't handle non-finite values.
Results may differ from a plain program's by a relative error of at most 0.017.
Values may be sent and summed in bfloat16 or wider, within the bound.
A program may use at most 64 MiB of HBM per device.

v0:
```python
import jax
import jax.numpy as jnp
from jax import lax
from jax.sharding import PartitionSpec as P

MOMENT_RATE = 0.9
OUTER_RATE = 0.7
NORM_EPS = 1e-05


def outer_step(partner, pseudo_grad, momentum, outer_params):
    replicas = lax.axis_size("replica")
    flat_grad = pseudo_grad.reshape(replicas, pseudo_grad.size // replicas)
    received = lax.all_to_all(flat_grad, "replica", split_axis=0, concat_axis=0, tiled=True)
    mirror = jnp.take(received, partner, axis=0)
    local_mean = (received.astype(jnp.float32) + mirror.astype(jnp.float32)) * 0.5
    pair_mean = lax.all_to_all(local_mean, "replica", split_axis=0, concat_axis=0, tiled=True)
    pair_mean = pair_mean.reshape(pseudo_grad.shape)
    moment = MOMENT_RATE * momentum.astype(jnp.float32) + pair_mean
    fresh = outer_params.astype(jnp.float32) - OUTER_RATE * (pair_mean + MOMENT_RATE * moment)
    return (fresh.astype(jnp.bfloat16), moment.astype(jnp.bfloat16))


def layer_pass(activations, norm_gain, key_weight, key_cotangent):
    acts = activations[0]
    gain = norm_gain[0]
    shard_weight = key_weight[0]
    cotangent = key_cotangent[0]
    wide_acts = acts.astype(jnp.float32)
    inv_rms = lax.rsqrt(jnp.mean(wide_acts * wide_acts, axis=-1, keepdims=True) + NORM_EPS)
    normed = (wide_acts * inv_rms * gain).astype(jnp.bfloat16)
    transpose_dims = (((1,), (1,)), ((), ()))
    columns = normed
    key_total = jnp.dot(
        columns,
        lax.all_gather(shard_weight, "fsdp", axis=0, tiled=True),
        preferred_element_type=jnp.float32,
    )
    normed_grad = lax.dot_general(
        cotangent,
        lax.all_gather(shard_weight, "fsdp", axis=0, tiled=True),
        transpose_dims,
        preferred_element_type=jnp.float32,
    )
    columns = normed
    weight_sum = lax.psum_scatter(
        lax.dot_general(
            columns, cotangent, (((0,), (0,)), ((), ())), preferred_element_type=jnp.float32
        ).astype(jnp.bfloat16),
        "fsdp",
        scatter_dimension=0,
        tiled=True,
    )
    gain_local = jnp.sum(normed_grad * wide_acts * inv_rms, axis=0)
    gain_total = lax.psum(gain_local, "fsdp")
    return (key_total.astype(jnp.bfloat16)[None], weight_sum[None], gain_total[None])


def body(
    partner, pseudo_grad, momentum, outer_params, activations, norm_gain, key_weight, key_cotangent
):
    key_out, grad_out, gain_out = layer_pass(activations, norm_gain, key_weight, key_cotangent)
    fresh, moment = outer_step(partner, pseudo_grad, momentum, outer_params)
    return (fresh, moment, key_out, grad_out, gain_out)


def solution(mesh):
    in_specs = (
        P(),
        P("replica", "fsdp", None),
        P("replica", "fsdp", None),
        P("replica", "fsdp", None),
        P("replica", "fsdp", None),
        P("replica", None),
        P("replica", "fsdp", None),
        P("replica", "fsdp", None),
    )
    out_specs = (
        P("replica", "fsdp", None),
        P("replica", "fsdp", None),
        P("replica", "fsdp", None),
        P("replica", "fsdp", None),
        P("replica", None),
    )
    return jax.shard_map(body, mesh=mesh, in_specs=in_specs, out_specs=out_specs, check_vma=False)
```

profile of v0, /device:TPU:1, one launch (start us, length us, event | category | flops | bytes accessed | tf_op | source)
XLA Modules:
  0.0 172.0 jit_solution(6828472801822279240)
XLA Ops:
  7.2 0.7 all-gather.3.cloned.1.call-update
  7.9 0.0 reduce-scatter.2.cloned.1.call-start
  8.0 1.5 fusion.6
  9.5 4.1 %convolution_convert_fusion = bf16[4096,512]{1,0:T(8,128)(2,1)} fusion(bf16[1,128,4096]{2,1,0:T(8,128)(2,1)S(1)} %copy-done.1, f32[4096]{0:T(1024)} %bitcast.49, f32[128]{0:T(128)S(1)} %add_rsqrt_fusion, bf16[1,128,512]{2,1,0:T(8,128)(2,1)S(1)} %copy-done), kind=kOutput, calls=%fused_computation.1 | convolution fusion | flops 541065216 | bytes 5390848 | tf_op jit(solution)/shard_map/dot_general | solution.py:47
  13.6 1.0 copy-done.2
  14.6 0.3 all_to_all.16
  14.9 0.5 broadcast.54
  15.4 3.9 %reduce.1 = bf16[64,4096]{1,0:T(8,128)(2,1)S(1)} reduce(bf16[64,1,4096]{2,1,0:T(2,128)(2,1)S(1)} %all_to_all.16, bf16[]{:T(256)} %broadcast.54), dimensions={1}, to_apply=%all_to_all.16.reduce_sub_computation | reduce | bytes 1048578 | tf_op jit(solution)/shard_map/all_to_all | solution.py:14
  19.4 1.2 reshape.89
  20.6 19.6 %all-to-all-start = ((bf16[64,2,2048]{2,1,0:T(2,128)(2,1)}), bf16[64,2,2048]{2,1,0:T(2,128)(2,1)S(1)}, u32[]{:S(2)}, u32[]{:S(2)}) async-start(bf16[64,2,2048]{2,1,0:T(2,128)(2,1)} %reshape.89), calls=%async_computation | async-start | bytes 1048576 | tf_op jit(solution)/shard_map/all_to_all | solution.py:14
  40.2 19.6 %all-to-all-done = bf16[64,2,2048]{2,1,0:T(2,128)(2,1)S(1)} async-done(((bf16[64,2,2048]{2,1,0:T(2,128)(2,1)}), bf16[64,2,2048]{2,1,0:T(2,128)(2,1)S(1)}, u32[]{:S(2)}, u32[]{:S(2)}) %all-to-all-start) | async-done | bytes 524320 | tf_op jit(solution)/shard_map/all_to_all | solution.py:14
  59.8 0.5 reshape.90
  60.3 0.6 copy.21
  60.9 0.9 gather_fusion
  61.8 0.8 add_multiply_fusion
  62.6 1.1 copy.17
  63.7 38.4 %all_to_all.19 = f32[64,1,4096]{2,1,0:T(1,128)S(1)} all-to-all(f32[64,1,4096]{2,1,0:T(1,128)S(1)} %copy.17), channel_id=1, replica_groups=mesh['replica'=64,'fsdp'=8] {'replica'}, dimensions={0} | all-to-all | bytes 2097152 | tf_op jit(solution)/shard_map/all_to_all | solution.py:17
  102.1 2.7 %reduce = f32[64,4096]{1,0:T(8,128)S(1)} reduce(f32[64,1,4096]{2,1,0:T(1,128)S(1)} %all_to_all.19, f32[]{:T(128)} %constant.36), dimensions={1}, to_apply=%all_to_all.15.reduce_sub_computation | reduce | bytes 2097156 | tf_op jit(solution)/shard_map/all_to_all | solution.py:17
  104.8 0.2 reshape.76
  105.0 2.5 %fusion.27 = (bf16[1,512,512]{2,1,0:T(8,128)(2,1)}, bf16[1,512,512]{2,1,0:T(8,128)(2,1)}) fusion(f32[1,512,512]{2,1,0:T(8,128)S(1)} %reshape.76, bf16[1,512,512]{2,1,0:T(8,128)(2,1)} %param.10, bf16[1,512,512]{2,1,0:T(8,128)(2,1)} %param.11), kind=kLoop, calls=%fused_computation.26 | loop fusion | flops 2621440 | bytes 3145728 | tf_op jit(solution)/shard_map/convert_element_type | solution.py:21
  107.5 3.7 %fusion.11 = f32[4096]{0:T(1024)S(1)} fusion(bf16[1,128,4096]{2,1,0:T(8,128)(2,1)S(1)} %copy-done.1, bf16[1,4096,512]{2,1,0:T(8,128)(2,1)} %all-gather.3.cloned.1.call-done, f32[128]{0:T(128)S(1)} %add_rsqrt_fusion, bf16[1,128,512]{2,1,0:T(8,128)(2,1)S(1)} %copy-done), kind=kOutput, calls=%fused_computation.16 | convolution fusion | flops 538963968 | bytes 5390848 | tf_op jit(solution)/shard_map/dot_general | solution.py:39
  111.2 25.2 %psum.7 = f32[1,4096]{1,0:T(1,128)} all-reduce(f32[1,4096]{1,0:T(1,128)S(1)} %bitcast.51), channel_id=1, replica_groups=mesh['replica'=64,'fsdp'=8] {'fsdp'}, use_global_device_ids=true, to_apply=%region_3.0 | all-reduce | flops 4096 | bytes 32768 | tf_op jit(solution)/shard_map/psum | solution.py:55
  136.4 3.7 %fusion.17 = bf16[1,128,512]{2,1,0:T(8,128)(2,1)} fusion(bf16[1,4096,512]{2,1,0:T(8,128)(2,1)} %all-gather.3.cloned.1.call-done, bf16[1,128,4096]{2,1,0:T(8,128)(2,1)S(1)} %copy-done.1, f32[4096]{0:T(1024)S(1)} %bitcast.50, f32[128]{0:T(128)S(1)} %add_rsqrt_fusion), kind=kOutput, calls=%fused_computation.18 | convolution fusion | flops 539033600 | bytes 5390848 | tf_op jit(solution)/shard_map/dot_general | solution.py:34
  140.1 25.1 %reduce-scatter.2.cloned.1.call-done = bf16[512,512]{1,0:T(8,128)(2,1)} async-done(((bf16[4096,512]{1,0:T(8,128)(2,1)}), bf16[512,512]{1,0:T(8,128)(2,1)}) %reduce-scatter.2.cloned.1.call-update) | async-done | bytes 524304 | tf_op jit(solution)/shard_map/reduce_scatter | solution.py:46
  (16 shorter events, 0.1 us)
Async XLA Ops:
  7.2 2.3 %copy-start = (bf16[1,128,512]{2,1,0:T(8,128)(2,1)S(1)}, bf16[1,128,512]{2,1,0:T(8,128)(2,1)}, u32[]{:S(2)}) copy-start(bf16[1,128,512]{2,1,0:T(8,128)(2,1)} %param.15) | copy-start | bytes 393220
  7.2 2.3 %copy-start.1 = (bf16[1,128,4096]{2,1,0:T(8,128)(2,1)S(1)}, bf16[1,128,4096]{2,1,0:T(8,128)(2,1)}, u32[]{:S(2)}) copy-start(bf16[1,128,4096]{2,1,0:T(8,128)(2,1)} %param.12) | copy-start | bytes 3145732
  7.2 100.3 %all-gather.3.cloned.1.call-start = ((), (), s32[]{:S(2)}) async-start(), calls=%async_computation.4 | async-start | bytes 4718592 | tf_op jit(solution)/shard_map/all_gather | solution.py:36
  7.9 157.2 %reduce-scatter.2.cloned.1.call-start = ((), (), s32[]{:S(2)}) async-start(), calls=%async_computation.3 | async-start | bytes 4718592 | tf_op jit(solution)/shard_map/reduce_scatter | solution.py:46
  13.6 1.0 copy-start.2
  14.9 25.2 %copy-start.4 = (s32[64]{0:T(128)S(1)}, s32[64]{0:T(128)}, u32[]{:S(2)}) copy-start(s32[64]{0:T(128)} %param.8) | copy-start | bytes 772
  20.6 39.2 %all-to-all-start = ((bf16[64,2,2048]{2,1,0:T(2,128)(2,1)}), bf16[64,2,2048]{2,1,0:T(2,128)(2,1)S(1)}, u32[]{:S(2)}, u32[]{:S(2)}) async-start(bf16[64,2,2048]{2,1,0:T(2,128)(2,1)} %reshape.89), calls=%async_computation | async-start | bytes 1048576 | tf_op jit(solution)/shard_map/all_to_all | solution.py:14
  107.5 28.9 %copy-start.3 = (f32[1,4096]{1,0:T(1,128)S(1)}, f32[1,4096]{1,0:T(1,128)}, u32[]{:S(2)}) copy-start(f32[1,4096]{1,0:T(1,128)} %param.13) | copy-start | bytes 49156
Sparse Core Ops, SparseCore 0:
  10.1 94.5 all-gather.2
  108.1 56.9 reduce-scatter.1
where the time goes:
time: 174 us; the launch traced here: 172 us
  blocking collectives  63.6 us (37%)
  waiting for transfers between devices  45.4 us (26%)
  starting transfers between devices  19.6 us (11%)
  between operations  14.2 us (8%)
  other arithmetic  11.5 us (7%)
  matrix products  11.4 us (7%)
  local copies, waits for them, and re-layouts  6.26 us (4%)
    all_to_all x1, blocking collectives, outer_step(): lax.all_to_all(local_mean, 'replica', split_axis=0, concat_axis=0, tiled=...  38.4 us
    psum x1, blocking collectives, layer_pass(): gain_total = lax.psum(gain_local, 'fsdp')  25.2 us
    reduce_scatter x1, waiting for transfers between devices, layer_pass(): lax.psum_scatter(lax.dot_general(columns, cotangent, (((0,), (0,)), ((),...  25.1 us
    all_to_all x1, waiting for transfers between devices, outer_step(): lax.all_to_all(flat_grad, 'replica', split_axis=0, concat_axis=0, tiled=T...  19.6 us
    all_to_all x1, starting transfers between devices, outer_step(): lax.all_to_all(flat_grad, 'replica', split_axis=0, concat_axis=0, tiled=T...  19.6 us
    dot_general x1, matrix products, layer_pass(): lax.dot_general(columns, cotangent, (((0,), (0,)), ((), ())), preferred_e...  4.06 us
    all_to_all x1, other arithmetic, outer_step(): lax.all_to_all(flat_grad, 'replica', split_axis=0, concat_axis=0, tiled=T...  3.94 us
    dot_general x1, matrix products, layer_pass(): lax.dot_general(cotangent, lax.all_gather(shard_weight, 'fsdp', axis=0, t...  3.68 us
  transfers between devices with their start and end apart: 3, of which 2 were waited for; matrix products, arithmetic and copies ran while one was open for 16% of the time, Pallas kernels for 0%

commit v1 on v0

v1 whole, which is shorter than its diff:
```python
import jax
import jax.numpy as jnp
from jax import lax
from jax.experimental import pallas as pl
from jax.experimental.pallas import tpu as pltpu
from jax.sharding import PartitionSpec as P

MOMENT_RATE = 0.9
OUTER_RATE = 0.7
NORM_EPS = 1e-05

MESH = pl.DeviceIdType.MESH
NX, NY = 4, 8
NQ = NX * NY
NP = 4
NF = 2 * NP
TOK = 128
D = 4096
BLK = D // NF
KC = 512
CUTS = 2
CW = KC // CUTS
ROWS = BLK // NQ

bf16 = jnp.bfloat16
f32 = jnp.float32


def body_kernel(
    partner, grad_h, mom_h, par_h, act_h, gain_v, w_h, cot_h,
    fresh_h, moment_h, keys_h, wgrad_h, ggrad_h,
    grad_v, mom_v, par_v, act_v, w_v, cot_v,
    met, back, mirror,
    acts, cots, x_in, x_out, u_in, u_out, d_in, d_out, own_part,
    wide_w, gcol, keys_v, wgrad_v, ggrad_v, fresh_v, moment_v, rms_v,
    load_sem, out_sem, one_send, one_recv, z_send, z_recv, two_send, two_recv,
    act_send, act_recv, cu_send, cd_send, cx_send, c_recv,
    x_send, x_recv, u_send, u_recv, d_send, d_recv, g_send, g_recv,
):
    r = lax.axis_index("replica")
    f = lax.axis_index("fsdp")
    q = r // 2
    half = r % 2
    qx, qy = q // NY, q % NY
    p = f // 2
    c = f % 2

    def at(chip, core):
        return (r, chip * 2 + core)

    def peer(k):
        px = (qx + k // NY) % NX
        py = (qy + k % NY) % NY
        return px * NY + py

    def remote(src, dst, ss, rs, dev):
        return pltpu.make_async_remote_copy(
            src_ref=src, dst_ref=dst, send_sem=ss, recv_sem=rs, device_id=dev, device_id_type=MESH
        )

    loads = []
    for i, (src, dst) in enumerate(
        (
            (act_h.at[0], act_v),
            (grad_h.at[0], grad_v),
            (act_h.at[0, :, pl.ds(pl.multiple_of(f * BLK, BLK), BLK)], acts.at[f]),
            (cot_h.at[0], cot_v),
            (w_h.at[0], w_v),
            (mom_h.at[0], mom_v),
            (par_h.at[0], par_v),
        )
    ):
        cp = pltpu.make_async_copy(src, dst, load_sem.at[i])
        cp.start()
        loads.append(cp)

    barrier = pltpu.get_barrier_semaphore()

    def greet(k, carry):
        pl.semaphore_signal(barrier, inc=1, device_id=(peer(k) * 2 + half, f), device_id_type=MESH)
        return carry

    lax.fori_loop(1, NQ, greet, 0)
    pl.semaphore_signal(barrier, inc=1, device_id=(q * 2 + 1 - half, f), device_id_type=MESH)
    for k in range(1, NF):
        pl.semaphore_signal(barrier, inc=1, device_id=(r, (f + k) % NF), device_id_type=MESH)
    pl.semaphore_wait(barrier, NQ - 1 + 1 + NF - 1)

    loads[0].wait()
    for k in (4, 3, 5, 2, 6, 1, 7):
        to = (f + k) % NF
        remote(
            act_v.at[:, pl.ds(pl.multiple_of(to * BLK, BLK), BLK)], acts.at[f], act_send, act_recv.at[f], (r, to)
        ).start()

    loads[1].wait()
    for s in range(CUTS):

        def leg_one(k, carry, s=s):
            to = peer(k)
            remote(
                grad_v.at[pl.ds(pl.multiple_of(to * ROWS, ROWS), ROWS), pl.ds(s * CW, CW)],
                met[s].at[q], one_send.at[s], one_recv.at[s], (to * 2 + half, f),
            ).start()
            return carry

        lax.fori_loop(1, NQ, leg_one, 0)
        met[s][q] = grad_v[pl.ds(pl.multiple_of(q * ROWS, ROWS), ROWS), pl.ds(s * CW, CW)]

    def square(i, acc):
        a = act_v[:, pl.ds(pl.multiple_of(i * 512, 512), 512)].astype(f32)
        return acc + a * a

    total = lax.fori_loop(0, D // 512, square, jnp.zeros((TOK, 512), f32))
    inv_rms = lax.rsqrt(jnp.sum(total, axis=-1, keepdims=True) * (1.0 / D) + NORM_EPS)
    rms_v[...] = jnp.broadcast_to(inv_rms, (TOK, 128))

    loads[3].wait()
    cots[f] = (cot_v[...].astype(f32) * inv_rms).astype(bf16)

    def cot_up(b):
        return remote(cots.at[b * 2 + c], cots.at[b * 2 + c], cu_send.at[b], c_recv.at[b * 2 + c], at(p + 1, c))

    def cot_down(b):
        return remote(cots.at[b * 2 + c], cots.at[b * 2 + c], cd_send.at[b], c_recv.at[b * 2 + c], at(p - 1, c))

    def cot_across(b):
        return remote(cots.at[b * 2 + c], cots.at[b * 2 + c], cx_send.at[b], c_recv.at[b * 2 + c], at(p, 1 - c))

    @pl.when(p < NP - 1)
    def _():
        cot_up(p).start()

    @pl.when(p > 0)
    def _():
        cot_down(p).start()

    cot_across(p).start()

    gain = gain_v[:, pl.ds(pl.multiple_of(f * BLK, BLK), BLK)]
    gcol[...] = jnp.transpose(jnp.broadcast_to(gain, (128, BLK)))
    loads[4].wait()
    wide_w[...] = (w_v[...].astype(f32) * gcol[:, 0:1]).astype(bf16)

    def z_copy(s):
        return remote(
            met[s].at[pl.ds(0, NQ)], met[s].at[pl.ds(NQ, NQ)], z_send.at[s], z_recv.at[s], (q * 2 + 1 - half, f)
        )

    def all_but_one(ref, ss, rs):
        return remote(ref.at[pl.ds(0, NQ - 1)], ref.at[pl.ds(0, NQ - 1)], ss, rs, (r, f))

    for s in range(CUTS):
        all_but_one(met[s], one_send.at[s], one_recv.at[s]).wait_recv()
        z_copy(s).start()

    for k in range(1, NP):

        @pl.when(p >= k)
        def _(k=k):
            b = p - k
            cot_up(b).wait_recv()
            cot_across(b).start()

            @pl.when(p < NP - 1)
            def _():
                cot_up(b).start()

        @pl.when(p < NP - k)
        def _(k=k):
            b = p + k
            cot_down(b).wait_recv()
            cot_across(b).start()

            @pl.when(p > 0)
            def _():
                cot_down(b).start()

    def act_arrival(b):
        return remote(acts.at[b], acts.at[b], act_send, act_recv.at[b], (r, f))

    def across(j):
        return remote(x_out.at[j], x_in.at[j], x_send.at[j], x_recv.at[j], at(p, 1 - c))

    loads[2].wait()
    for k in range(NP):
        j = (p + k) % NP
        if k > 0:
            act_arrival(j * 2 + c).wait_recv()
        act_arrival(j * 2 + 1 - c).wait_recv()
        x_out[j] = jnp.dot(acts[j * 2 + 1 - c], wide_w[...], preferred_element_type=f32).astype(bf16)
        across(j).start()
        own_part[j] = jnp.dot(acts[j * 2 + c], wide_w[...], preferred_element_type=f32)

    def up(j):
        return remote(u_out.at[j], u_in.at[j], u_send.at[j], u_recv.at[j], at(p + 1, c))

    def down(j):
        return remote(d_out.at[j], d_in.at[j], d_send.at[j], d_recv.at[j], at(p - 1, c))

    for k in range(NP - 1, 0, -1):

        @pl.when(p + k < NP)
        def _(k=k):
            j = p + k
            across(j).wait_recv()

            @pl.when(p > 0)
            def _():
                up(j).wait_recv()
                u_out[j] = (own_part[j] + x_in[j].astype(f32) + u_in[j].astype(f32)).astype(bf16)

            @pl.when(p == 0)
            def _():
                u_out[j] = (own_part[j] + x_in[j].astype(f32)).astype(bf16)

            up(j).start()

        @pl.when(p - k >= 0)
        def _(k=k):
            j = p - k
            across(j).wait_recv()

            @pl.when(p < NP - 1)
            def _():
                down(j).wait_recv()
                d_out[j] = (own_part[j] + x_in[j].astype(f32) + d_in[j].astype(f32)).astype(bf16)

            @pl.when(p == NP - 1)
            def _():
                d_out[j] = (own_part[j] + x_in[j].astype(f32)).astype(bf16)

            down(j).start()

    for k in range(NP):
        across_block = ((p + k) % NP) * 2 + 1 - c
        remote(cots.at[across_block], cots.at[across_block], cx_send.at[0], c_recv.at[across_block], (r, f)).wait_recv()
    wide = 256
    for b in range(BLK // wide):
        lanes = pl.ds(b * wide, wide)
        a = acts[:, :, lanes].reshape(NF * TOK, wide)
        m = lax.dot_general(
            a, cots[...].reshape(NF * TOK, KC), (((0,), (0,)), ((), ())), preferred_element_type=f32
        )
        wgrad_v[lanes, :] = (m * gcol[lanes, 0:1]).astype(bf16)
        prod = m * w_v[lanes, :].astype(f32)
        folded = prod[:, 0:128]
        for e in range(1, KC // 128):
            folded = folded + prod[:, e * 128 : (e + 1) * 128]
        ggrad_v[:, pl.ds(pl.multiple_of(f * BLK + b * wide, wide), wide)] = jnp.sum(
            jnp.transpose(folded), axis=0, keepdims=True
        )
    mine = ggrad_v.at[:, pl.ds(pl.multiple_of(f * BLK, BLK), BLK)]
    for k in range(1, NF):
        remote(mine, mine, g_send, g_recv, (r, (f + k) % NF)).start()
    wgrad_out = pltpu.make_async_copy(wgrad_v, wgrad_h.at[0], out_sem.at[3])
    wgrad_out.start()

    for s in range(CUTS):
        z_copy(s).wait_recv()

        def choose(k, carry, s=s):
            to = peer(k)
            other = partner[to * 2 + half]
            back[s][to] = met[s][lax.rem(other + half, 2) * NQ + lax.div(other, 2)]
            remote(
                back[s].at[to], mirror[s].at[pl.ds(pl.multiple_of(q * ROWS, ROWS), ROWS)],
                two_send.at[s], two_recv.at[s], (to * 2 + half, f),
            ).start()
            return carry

        lax.fori_loop(1, NQ, choose, 0)
        other = partner[r]
        mirror[s][pl.ds(pl.multiple_of(q * ROWS, ROWS), ROWS), :] = met[s][
            lax.rem(other + half, 2) * NQ + lax.div(other, 2)
        ]

    across(p).wait_recv()
    total = own_part[p] + x_in[p].astype(f32)
    own_part[p] = total

    @pl.when(p > 0)
    def _():
        up(p).wait_recv()
        own_part[p] += u_in[p].astype(f32)

    @pl.when(p < NP - 1)
    def _():
        down(p).wait_recv()
        own_part[p] += d_in[p].astype(f32)

    keys_v[...] = (own_part[p] * rms_v[:, 0:1]).astype(bf16)
    keys_out = pltpu.make_async_copy(keys_v, keys_h.at[0], out_sem.at[2])
    keys_out.start()

    loads[5].wait()
    loads[6].wait()
    for s in range(CUTS):
        seen = remote(
            mirror[s].at[pl.ds(0, BLK - ROWS)], mirror[s].at[pl.ds(0, BLK - ROWS)], two_send.at[s], two_recv.at[s], (r, f)
        )
        seen.wait_recv()
        lanes = pl.ds(s * CW, CW)
        mean = (grad_v[:, lanes].astype(f32) + mirror[s][...].astype(f32)) * 0.5
        moment = MOMENT_RATE * mom_v[:, lanes].astype(f32) + mean
        moment_v[:, lanes] = moment.astype(bf16)
        fresh_v[:, lanes] = (
            par_v[:, lanes].astype(f32) - OUTER_RATE * (mean + MOMENT_RATE * moment)
        ).astype(bf16)
    fresh_out = pltpu.make_async_copy(fresh_v, fresh_h.at[0], out_sem.at[0])
    moment_out = pltpu.make_async_copy(moment_v, moment_h.at[0], out_sem.at[1])
    fresh_out.start()
    moment_out.start()

    seven = ggrad_v.at[:, pl.ds(0, D - BLK)]
    remote(seven, seven, g_send, g_recv, (r, f)).wait()
    ggrad_out = pltpu.make_async_copy(ggrad_v, ggrad_h, out_sem.at[4])
    ggrad_out.start()

    remote(acts.at[pl.ds(0, NF - 1)], acts.at[pl.ds(0, NF - 1)], act_send, act_recv.at[0], (r, f)).wait_send()
    for s in range(CUTS):
        all_but_one(met[s], one_send.at[s], one_recv.at[s]).wait_send()
        z_copy(s).wait_send()
        all_but_one(back[s], two_send.at[s], two_recv.at[s]).wait_send()
    for j in range(NP):
        across(j).wait_send()
        cot_across(j).wait_send()

        @pl.when((p >= j) & (p < NP - 1))
        def _(j=j):
            cot_up(j).wait_send()

        @pl.when((p <= j) & (p > 0))
        def _(j=j):
            cot_down(j).wait_send()

        @pl.when(j > p)
        def _(j=j):
            up(j).wait_send()

        @pl.when(j < p)
        def _(j=j):
            down(j).wait_send()

    for cp in (keys_out, wgrad_out, fresh_out, moment_out, ggrad_out):
        cp.wait()


def wrapped(*refs):
    n = 13 + 6
    head, rest = refs[:n], refs[n:]
    met, back, mirror = rest[:CUTS], rest[CUTS : 2 * CUTS], rest[2 * CUTS : 3 * CUTS]
    body_kernel(*head, met, back, mirror, *rest[3 * CUTS :])


def body(partner, pseudo_grad, momentum, outer_params, activations, norm_gain, key_weight, key_cotangent):
    hbm = pl.BlockSpec(memory_space=pl.ANY)
    vmem = pltpu.VMEM
    dma = pltpu.SemaphoreType.DMA
    tok_blocks = lambda n: vmem((n, TOK, KC), bf16)
    scratch = (
        [vmem((BLK, KC), bf16)] * 3
        + [vmem((TOK, D), bf16), vmem((BLK, KC), bf16), vmem((TOK, KC), bf16)]
        + [vmem((2 * NQ, ROWS, CW), bf16)] * CUTS
        + [vmem((NQ, ROWS, CW), bf16)] * CUTS
        + [vmem((BLK, CW), bf16)] * CUTS
        + [tok_blocks(NF), tok_blocks(NF)]
        + [tok_blocks(NP)] * 6
        + [vmem((NP, TOK, KC), f32)]
        + [
            vmem((BLK, KC), bf16),
            vmem((BLK, 128), f32),
            vmem((TOK, KC), bf16),
            vmem((BLK, KC), bf16),
            vmem((1, D), f32),
            vmem((BLK, KC), bf16),
            vmem((BLK, KC), bf16),
            vmem((TOK, 128), f32),
        ]
        + [dma((7,)), dma((5,))]
        + [dma((CUTS,))] * 6
        + [dma, dma((NF,)), dma((NP,)), dma((NP,)), dma((NP,)), dma((NF,))]
        + [dma((NP,))] * 6
        + [dma, dma]
    )
    return pl.pallas_call(
        wrapped,
        out_shape=(
            jax.ShapeDtypeStruct((1, BLK, KC), bf16),
            jax.ShapeDtypeStruct((1, BLK, KC), bf16),
            jax.ShapeDtypeStruct((1, TOK, KC), bf16),
            jax.ShapeDtypeStruct((1, BLK, KC), bf16),
            jax.ShapeDtypeStruct((1, D), f32),
        ),
        in_specs=[
            pl.BlockSpec(memory_space=pltpu.SMEM), hbm, hbm, hbm, hbm,
            pl.BlockSpec(memory_space=pltpu.VMEM), hbm, hbm,
        ],
        out_specs=[hbm] * 5,
        scratch_shapes=scratch,
        compiler_params=pltpu.CompilerParams(
            collective_id=0, has_side_effects=True, vmem_limit_bytes=62 * 2**20
        ),
        name="step",
    )(partner, pseudo_grad, momentum, outer_params, activations, norm_gain, key_weight, key_cotangent)


def solution(mesh):
    sharded = P("replica", "fsdp", None)
    in_specs = (P(), sharded, sharded, sharded, sharded, P("replica", None), sharded, sharded)
    out_specs = (sharded, sharded, sharded, sharded, P("replica", None))
    return jax.shard_map(body, mesh=mesh, in_specs=in_specs, out_specs=out_specs, check_vma=False)
```

time: 174 us -> 107 us (0.61)
  the two profiles are of different devices: /device:TPU:1 before, /device:TPU:128 now
where the time goes in v1:
time: 107 us
  Pallas kernels  102 us (95%)
  local copies, waits for them, and re-layouts  4.99 us (5%)
    pallas_call x1, Pallas kernels, body(): pl.pallas_call(wrapped, out_shape=(jax.ShapeDtypeStruct((1, BLK, KC), bf1...  102 us
    unnamed x13, local copies, waits for them, and re-layouts  4.99 us

profile of v1, /device:TPU:128, one launch (start us, length us, event | category | flops | bytes accessed | tf_op | source)
XLA Modules:
  0.0 107.2 jit_solution(4421147742606969789)
XLA Ops:
  0.6 101.5 %step.1 = (bf16[1,512,512]{2,1,0:T(8,128)(2,1)}, bf16[1,512,512]{2,1,0:T(8,128)(2,1)}, bf16[1,128,512]{2,1,0:T(8,128)(2,1)}, bf16[1,512,512]{2,1,0:T(8,128)(2,1)}, f32[1,4096]{1,0:T(1,128)}) custom-call(s32[64]{0:T(128)} %refs_0_.1, bf16[1,512,512]{2,1,0:T(8,128)(2,1)} %refs_1_.1, bf16[1,512,512]{2,1,0:T(8,128)(2,1)} %refs_2_.1, ...), custom_call_target="tpu_custom_call" | custom-call | tf_op jit(solution)/shard_map/step/pallas_call | solution.py:386
  102.2 0.0 copy-start.1
  102.2 1.9 %copy.18 = bf16[1,512,512]{2,1,0:T(8,128)(2,1)} copy(bf16[1,512,512]{2,1,0:T(8,128)(2,1)} %get-tuple-element.10) | data formatting | bytes 1048576
  104.1 0.0 copy-done.1
  104.1 0.0 copy-start.2
  104.1 0.0 copy-start
  104.1 0.8 copy.19
  104.9 0.2 copy-done.2
  105.1 0.7 copy.20
  105.8 0.0 copy-done
  105.8 0.0 copy-start.3
  105.8 0.8 copy.21
  106.6 0.0 copy-done.3
  106.6 0.6 copy.22
Async XLA Ops:
  102.2 1.9 %copy-start.1 = (bf16[1,512,512]{2,1,0:T(8,128)(2,1)S(1)}, bf16[1,512,512]{2,1,0:T(8,128)(2,1)}, u32[]{:S(2)}) copy-start(bf16[1,512,512]{2,1,0:T(8,128)(2,1)} %get-tuple-element.11) | copy-start | bytes 1572868
  104.1 1.0 copy-start.2
  104.1 1.7 %copy-start = (bf16[1,512,512]{2,1,0:T(8,128)(2,1)S(1)}, bf16[1,512,512]{2,1,0:T(8,128)(2,1)}, u32[]{:S(2)}) copy-start(bf16[1,512,512]{2,1,0:T(8,128)(2,1)} %get-tuple-element.13) | copy-start | bytes 1572868
  105.8 0.8 copy-start.3

commit v2 on v0

v2 whole, which is shorter than its diff:
```python
import functools

import jax
import jax.numpy as jnp
from jax import lax
from jax.experimental import pallas as pl
from jax.experimental.pallas import tpu as pltpu
from jax.sharding import PartitionSpec as P

MOMENT_RATE = 0.9
OUTER_RATE = 0.7
NORM_EPS = 1e-05

MESH = pl.DeviceIdType.MESH
NX, NY = 4, 8
NQ = NX * NY
REPS = 2 * NQ
NP = 4
NF = 2 * NP
TOK = 128
D = 4096
BLK = D // NF
KC = 512
CUTS = 4
CW = KC // CUTS
ROWS = BLK // NQ

bf16 = jnp.bfloat16
f32 = jnp.float32


def body_kernel(
    cap,
    partner_h, grad_h, mom_h, par_h, act_h, gain_h, w_h, cot_h,
    fresh_h, moment_h, keys_h, wgrad_h, ggrad_h,
    partner, gain_v, grad_v, mom_v, par_v, act_v, w_v, cot_v,
    met, packed, beyond, back, mirror, fresh_v, moment_v,
    acts, cots, x_in, x_out, near_in, near_out, far_out, far_in, own_part,
    wide_w, gcol, keys_v, wgrad_v, ggrad_v, rms_v,
    load_sem, out_sem, one_send, one_recv, z_send, z_recv, two_send, two_recv,
    act_send, act_recv, cu_send, cd_send, cx_send, c_recv,
    x_send, x_recv, n_send, n_recv, f_send, f_recv, g_send, g_recv,
):
    r = lax.axis_index("replica")
    f = lax.axis_index("fsdp")
    q = r // 2
    half = r % 2
    qx, qy = q // NY, q % NY
    p = f // 2
    c = f % 2

    def at(chip, core):
        return (r, chip * 2 + core)

    def peer(k):
        px = (qx + k // NY) % NX
        py = (qy + k % NY) % NY
        return px * NY + py

    def remote(src, dst, ss, rs, dev):
        return pltpu.make_async_remote_copy(
            src_ref=src, dst_ref=dst, send_sem=ss, recv_sem=rs, device_id=dev, device_id_type=MESH
        )

    def rows_of(i):
        return pl.ds(pl.multiple_of(i * ROWS, ROWS), ROWS)

    def block_of(i):
        return pl.ds(pl.multiple_of(i * BLK, BLK), BLK)

    barrier = pltpu.get_barrier_semaphore()
    loads = [
        pltpu.make_async_copy(src, dst, load_sem.at[i])
        for i, (src, dst) in enumerate(
            (
                (act_h.at[0], act_v),
                (cot_h.at[0], cot_v),
                (gain_h, gain_v),
                (w_h.at[0], w_v),
                (grad_h.at[0], grad_v),
                (act_h.at[0, :, block_of(f)], acts.at[f]),
                (partner_h, partner),
                (mom_h.at[0], mom_v),
                (par_h.at[0], par_v),
            )
        )
    ]

    def act_copy(to):
        return remote(act_v.at[:, block_of(to)], acts.at[f], act_send, act_recv.at[f], (r, to))

    def act_arrival(b):
        return remote(acts.at[b], acts.at[b], act_send, act_recv.at[b], (r, f))

    def cot_up(b):
        return remote(cots.at[b * 2 + c], cots.at[b * 2 + c], cu_send.at[b], c_recv.at[b * 2 + c], at(p + 1, c))

    def cot_down(b):
        return remote(cots.at[b * 2 + c], cots.at[b * 2 + c], cd_send.at[b], c_recv.at[b * 2 + c], at(p - 1, c))

    def cot_across(b):
        return remote(cots.at[b * 2 + c], cots.at[b * 2 + c], cx_send.at[b], c_recv.at[b * 2 + c], at(p, 1 - c))

    def cot_arrival(b):
        return remote(cots.at[b], cots.at[b], cx_send.at[0], c_recv.at[b], (r, f))

    def z_copy(s):
        return remote(met[s], beyond[s], z_send.at[s], z_recv.at[s], (q * 2 + 1 - half, f))

    def all_but_one(ref, ss, rs):
        return remote(ref.at[pl.ds(0, NQ - 1)], ref.at[pl.ds(0, NQ - 1)], ss, rs, (r, f))

    def across(j):
        return remote(x_out.at[j], x_in.at[j], x_send.at[j], x_recv.at[j], at(p, 1 - c))

    near_chip = p + 1 - 2 * (p % 2)
    edge, inner = p % 3 == 0, p % 3 > 0
    far_chips = (3 - 3 * (p // 2), 2 - p // 2)

    def near(j):
        return remote(near_out.at[j], near_in.at[j], n_send.at[j], n_recv.at[j], at(near_chip, c))

    def far(j):
        return remote(far_out.at[j], far_in, f_send.at[j], f_recv, at(j, c))

    def load_and_greet():
        for cp in loads:
            cp.start()

        def greet(k, carry):
            pl.semaphore_signal(barrier, inc=1, device_id=(peer(k) * 2 + half, f), device_id_type=MESH)
            return carry

        lax.fori_loop(1, NQ, greet, 0)
        pl.semaphore_signal(barrier, inc=1, device_id=(q * 2 + 1 - half, f), device_id_type=MESH)
        for k in range(1, NF):
            pl.semaphore_signal(barrier, inc=1, device_id=(r, (f + k) % NF), device_id_type=MESH)

    def norm():
        loads[0].wait()

        def square(i, acc):
            a = act_v[:, pl.ds(pl.multiple_of(i * 512, 512), 512)].astype(f32)
            return acc + a * a

        total = lax.fori_loop(0, D // 512, square, jnp.zeros((TOK, 512), f32))
        inv_rms = lax.rsqrt(jnp.sum(total, axis=-1, keepdims=True) * (1.0 / D) + NORM_EPS)
        rms_v[...] = jnp.broadcast_to(inv_rms, (TOK, 128))
        loads[1].wait()
        cots[f] = (cot_v[...].astype(f32) * inv_rms).astype(bf16)
        loads[2].wait()
        gcol[...] = jnp.transpose(jnp.broadcast_to(gain_v[:, block_of(f)], (128, BLK)))
        loads[3].wait()
        wide_w[...] = (w_v[...].astype(f32) * gcol[:, 0:1]).astype(bf16)
        loads[4].wait()

    def leg_one():
        for s in range(CUTS):

            def send(k, carry, s=s):
                to = peer(k)
                remote(
                    grad_v.at[rows_of(to), pl.ds(s * CW, CW)],
                    met[s].at[q], one_send.at[s], one_recv.at[s], (to * 2 + half, f),
                ).start()
                return carry

            lax.fori_loop(1, NQ, send, 0)
            met[s][q] = grad_v[rows_of(q), pl.ds(s * CW, CW)]

    def crossing(i, side):
        return lax.rem(partner[i * 2 + side] + side, 2)

    def tables():
        loads[6].wait()

    def leg_z(s):
        all_but_one(met[s], one_send.at[s], one_recv.at[s]).wait_recv()

        z_copy(s).start()

    def leg_two(s):
        z_copy(s).wait_recv()

        def mirror_of(to):
            other = partner[to * 2 + half]
            i = lax.div(other, 2)
            here = met[s][i]
            there = beyond[s][i]
            return jnp.where(lax.rem(other + half, 2) == 1, there, here)

        def send(k, carry):
            to = peer(k)
            back[s][to] = mirror_of(to)
            remote(
                back[s].at[to], mirror[s].at[rows_of(q)], two_send.at[s], two_recv.at[s], (to * 2 + half, f)
            ).start()
            return carry

        lax.fori_loop(1, NQ, send, 0)
        mirror[s][rows_of(q), :] = mirror_of(q)

    def outer_step(s):
        remote(
            mirror[s].at[pl.ds(0, BLK - ROWS)], mirror[s].at[pl.ds(0, BLK - ROWS)],
            two_send.at[s], two_recv.at[s], (r, f),
        ).wait_recv()
        lanes = pl.ds(s * CW, CW)
        mean = (grad_v[:, lanes].astype(f32) + mirror[s][...].astype(f32)) * 0.5
        moment = MOMENT_RATE * mom_v[:, lanes].astype(f32) + mean
        moment_v[s][...] = moment.astype(bf16)
        fresh_v[s][...] = (
            par_v[:, lanes].astype(f32) - OUTER_RATE * (mean + MOMENT_RATE * moment)
        ).astype(bf16)
        step_out[2 * s].start()
        step_out[2 * s + 1].start()

    def cots_begin():
        @pl.when(p < NP - 1)
        def _():
            cot_up(p).start()

        @pl.when(p > 0)
        def _():
            cot_down(p).start()

        cot_across(p).start()

    def cots_onward(k):
        @pl.when(p >= k)
        def _():
            b = p - k
            cot_up(b).wait_recv()
            cot_across(b).start()

            @pl.when(p < NP - 1)
            def _():
                cot_up(b).start()

        @pl.when(p < NP - k)
        def _():
            b = p + k
            cot_down(b).wait_recv()
            cot_across(b).start()

            @pl.when(p > 0)
            def _():
                cot_down(b).start()

    def partial_keys(j, own):
        if own:
            loads[5].wait()
        else:
            act_arrival(j * 2 + c).wait_recv()
        act_arrival(j * 2 + 1 - c).wait_recv()
        x_out[j] = jnp.dot(acts[j * 2 + 1 - c], wide_w[...], preferred_element_type=f32).astype(bf16)
        across(j).start()
        own_part[j] = jnp.dot(acts[j * 2 + c], wide_w[...], preferred_element_type=f32)

    def sum_near(j):
        across(j).wait_recv()
        near_out[j] = (own_part[j] + x_in[j].astype(f32)).astype(bf16)
        near(j).start()

    def sum_far(j):
        across(j).wait_recv()
        near(j).wait_recv()
        far_out[j] = (own_part[j] + x_in[j].astype(f32) + near_in[j].astype(f32)).astype(bf16)
        far(j).start()

    keys_out = pltpu.make_async_copy(keys_v, keys_h.at[0], out_sem.at[0])
    wgrad_out = pltpu.make_async_copy(wgrad_v, wgrad_h.at[0], out_sem.at[1])
    ggrad_out = pltpu.make_async_copy(ggrad_v, ggrad_h, out_sem.at[2])
    step_out = []
    for s in range(CUTS):
        step_out.append(pltpu.make_async_copy(fresh_v[s], fresh_h.at[s], out_sem.at[3 + s]))
        step_out.append(pltpu.make_async_copy(moment_v[s], moment_h.at[s], out_sem.at[3 + CUTS + s]))

    def finish_keys():
        across(p).wait_recv()
        near(p).wait_recv()
        total = own_part[p] + x_in[p].astype(f32) + near_in[p].astype(f32)
        far(p).wait_recv()
        keys_v[...] = ((total + far_in[...].astype(f32)) * rms_v[:, 0:1]).astype(bf16)
        keys_out.start()

    def weight_grad():
        for k in range(NP):
            cot_arrival(((p + k) % NP) * 2 + 1 - c).wait_recv()
        wide = 256
        for b in range(BLK // wide):
            lanes = pl.ds(b * wide, wide)
            a = acts[:, :, lanes].reshape(NF * TOK, wide)
            m = lax.dot_general(
                a, cots[...].reshape(NF * TOK, KC), (((0,), (0,)), ((), ())), preferred_element_type=f32
            )
            wgrad_v[lanes, :] = (m * gcol[lanes, 0:1]).astype(bf16)
            prod = m * w_v[lanes, :].astype(f32)
            folded = prod[:, 0:128]
            for e in range(1, KC // 128):
                folded = folded + prod[:, e * 128 : (e + 1) * 128]
            ggrad_v[:, pl.ds(pl.multiple_of(f * BLK + b * wide, wide), wide)] = jnp.sum(
                jnp.transpose(folded), axis=0, keepdims=True
            )
        mine = ggrad_v.at[:, block_of(f)]
        for k in range(1, NF):
            remote(mine, mine, g_send, g_recv, (r, (f + k) % NF)).start()
        wgrad_out.start()

    def finish_gain():
        seven = ggrad_v.at[:, pl.ds(0, D - BLK)]
        remote(seven, seven, g_send, g_recv, (r, f)).wait()
        ggrad_out.start()

    def drain():
        remote(acts.at[pl.ds(0, NF - 1)], acts.at[pl.ds(0, NF - 1)], act_send, act_recv.at[0], (r, f)).wait_send()
        for s in range(CUTS):
            all_but_one(met[s], one_send.at[s], one_recv.at[s]).wait_send()
            z_copy(s).wait_send()
            all_but_one(back[s], two_send.at[s], two_recv.at[s]).wait_send()
        for j in range(NP):
            across(j).wait_send()
            cot_across(j).wait_send()

            @pl.when((p >= j) & (p < NP - 1))
            def _(j=j):
                cot_up(j).wait_send()

            @pl.when((p <= j) & (p > 0))
            def _(j=j):
                cot_down(j).wait_send()

        near(near_chip).wait_send()
        for j in far_chips:

            @pl.when(edge)
            def _(j=j):
                near(j).wait_send()

            @pl.when(inner)
            def _(j=j):
                far(j).wait_send()

        for cp in (keys_out, wgrad_out, ggrad_out, *step_out):
            cp.wait()

    scope = jax.named_scope
    with scope("load"):
        load_and_greet()
    with scope("greet"):
        pl.semaphore_wait(barrier, NQ - 1 + 1 + NF - 1)
    with scope("norm"):
        norm()
    with scope("send_acts"):
        cots_begin()
        act_copy(p * 2 + 1 - c).start()
        for chip in (*far_chips, near_chip):
            for core in (c, 1 - c):
                act_copy(chip * 2 + core).start()
    with scope("leg_one"):
        leg_one()
    with scope("tables"):
        tables()
    with scope("cots_1"):
        cots_onward(1)
    with scope("leg_z_0"):
        leg_z(0)
    with scope("leg_z_1"):
        leg_z(1)
    with scope("leg_z_2"):
        leg_z(2)
    with scope("leg_z_3"):
        leg_z(3)
    with scope("wait_loads"):
        loads[7].wait()
        loads[8].wait()
    with scope("leg_two_0"):
        leg_two(0)
    with scope("leg_two_1"):
        leg_two(1)
    with scope("partial_keys_own"):
        partial_keys(p, True)
    with scope("partial_keys_far_1"):
        partial_keys(far_chips[0], False)
    with scope("sum_edge_1"):
        @pl.when(edge)
        def _():
            sum_near(far_chips[0])
    with scope("partial_keys_far_2"):
        partial_keys(far_chips[1], False)
    with scope("sum_edge_2"):
        @pl.when(edge)
        def _():
            sum_near(far_chips[1])
    with scope("cots_2"):
        cots_onward(2)
    with scope("sum_inner_1"):
        @pl.when(inner)
        def _():
            sum_far(far_chips[0])
    with scope("sum_inner_2"):
        @pl.when(inner)
        def _():
            sum_far(far_chips[1])
    with scope("leg_two_2"):
        leg_two(2)
    with scope("partial_keys_near"):
        partial_keys(near_chip, False)
    with scope("sum_near"):
        sum_near(near_chip)
    with scope("leg_two_3"):
        leg_two(3)
    with scope("cots_3"):
        cots_onward(3)
    with scope("weight_grad"):
        weight_grad()
    with scope("outer_step_0"):
        outer_step(0)
    with scope("outer_step_1"):
        outer_step(1)
    with scope("outer_step_2"):
        outer_step(2)
    with scope("finish_keys"):
        finish_keys()
    with scope("outer_step_3"):
        outer_step(3)
    with scope("finish_gain"):
        finish_gain()
    with scope("drain"):
        drain()

def wrapped(cap, *refs):
    n = 13 + 8
    head, rest = refs[:n], refs[n:]
    parts = [rest[i * CUTS : (i + 1) * CUTS] for i in range(7)]
    body_kernel(cap, *head, *parts, *rest[7 * CUTS :])


def hand_over(
    fresh_p, moment_p, keys_h, wgrad_h, ggrad_h, fresh_o, moment_o, keys_o, wgrad_o, ggrad_o,
    fresh_a, moment_a, keys_v, wgrad_v, ggrad_v, fresh_v, moment_v, arrive, leave,
):
    inward = [
        pltpu.make_async_copy(src, dst, arrive.at[i])
        for i, (src, dst) in enumerate(
            ((wgrad_h, wgrad_v), (keys_h, keys_v), (ggrad_h, ggrad_v), (fresh_p, fresh_a), (moment_p, moment_a))
        )
    ]
    outward = [
        pltpu.make_async_copy(src, dst, leave.at[i])
        for i, (src, dst) in enumerate(
            ((wgrad_v, wgrad_o), (keys_v, keys_o), (ggrad_v, ggrad_o), (fresh_v, fresh_o), (moment_v, moment_o))
        )
    ]
    for cp in inward:
        cp.start()
    for i in range(5):
        inward[i].wait()
        if i >= 3:
            parts, whole = ((fresh_a, fresh_v), (moment_a, moment_v))[i - 3]
            for s in range(CUTS):
                whole[0, :, pl.ds(s * CW, CW)] = parts[s]
        outward[i].start()
    for cp in outward:
        cp.wait()


def body(partner, pseudo_grad, momentum, outer_params, activations, norm_gain, key_weight, key_cotangent):
    hbm = pl.BlockSpec(memory_space=pl.ANY)
    vmem = pltpu.VMEM
    dma = pltpu.SemaphoreType.DMA
    tok_blocks = lambda n: vmem((n, TOK, KC), bf16)
    parts = (jax.ShapeDtypeStruct((CUTS, BLK, CW), bf16),) * 2
    results = (
        jax.ShapeDtypeStruct((1, BLK, KC), bf16),
        jax.ShapeDtypeStruct((1, BLK, KC), bf16),
        jax.ShapeDtypeStruct((1, TOK, KC), bf16),
        jax.ShapeDtypeStruct((1, BLK, KC), bf16),
        jax.ShapeDtypeStruct((1, D), f32),
    )

    def step(cap, collective_id):
        scratch = (
            [pltpu.SMEM((REPS,), jnp.int32), vmem((1, D), f32)]
            + [vmem((BLK, KC), bf16)] * 3
            + [vmem((TOK, D), bf16), vmem((BLK, KC), bf16), vmem((TOK, KC), bf16)]
            + [vmem((NQ, ROWS, CW), bf16)] * CUTS
            + [vmem((cap, ROWS, CW), bf16)] * (2 * CUTS)
            + [vmem((NQ, ROWS, CW), bf16)] * CUTS
            + [vmem((BLK, CW), bf16)] * (3 * CUTS)
            + [tok_blocks(NF), tok_blocks(NF)]
            + [tok_blocks(NP)] * 5
            + [vmem((TOK, KC), bf16)]
            + [vmem((NP, TOK, KC), f32)]
            + [
                vmem((BLK, KC), bf16),
                vmem((BLK, 128), f32),
                vmem((TOK, KC), bf16),
                vmem((BLK, KC), bf16),
                vmem((1, D), f32),
                vmem((TOK, 128), f32),
            ]
            + [dma((9,)), dma((3 + 2 * CUTS,))]
            + [dma((CUTS,))] * 6
            + [dma, dma((NF,)), dma((NP,)), dma((NP,)), dma((NP,)), dma((NF,))]
            + [dma((NP,))] * 5
            + [dma, dma, dma]
        )
        return pl.pallas_call(
            functools.partial(wrapped, cap),
            out_shape=parts + results[2:],
            in_specs=[hbm] * 8,
            out_specs=[hbm] * 5,
            scratch_shapes=scratch,
            compiler_params=pltpu.CompilerParams(
                collective_id=collective_id, has_side_effects=True, vmem_limit_bytes=62 * 2**20
            ),
            name=f"step_{cap}",
        )

    done = step(NQ, 0)(
        partner, pseudo_grad, momentum, outer_params, activations, norm_gain, key_weight, key_cotangent
    )
    return pl.pallas_call(
        hand_over,
        out_shape=results,
        in_specs=[hbm] * 5,
        out_specs=[hbm] * 5,
        scratch_shapes=[vmem(a.shape, a.dtype) for a in parts + results[2:] + results[:2]] + [dma((5,)), dma((5,))],
        compiler_params=pltpu.CompilerParams(vmem_limit_bytes=62 * 2**20),
        name="hand_over",
    )(*done)


def solution(mesh):
    sharded = P("replica", "fsdp", None)
    in_specs = (P(), sharded, sharded, sharded, sharded, P("replica", None), sharded, sharded)
    out_specs = (sharded, sharded, sharded, sharded, P("replica", None))
    return jax.shard_map(body, mesh=mesh, in_specs=in_specs, out_specs=out_specs, check_vma=False)
```

time: 174 us -> 81.6 us (0.47); the launches traced: 172 us -> 81.4 us
  Pallas kernels: 0 us -> 80.7 us
  blocking collectives: 63.6 us -> 0 us
  waiting for transfers between devices: 45.4 us -> 0 us
  starting transfers between devices: 19.6 us -> 0 us
  between operations: 14.2 us -> 0.64 us
  other arithmetic: 11.5 us -> 0 us
  matrix products: 11.4 us -> 0 us
  local copies, waits for them, and re-layouts: 6.26 us -> 0 us
    pallas_call x0 -> x2, Pallas kernels: none -> 80.7 us  [the longest x1 78.3 us: body(): step(NQ, 0)]
    all_to_all x1 -> x0, blocking collectives: 38.4 us -> none  [outer_step(): lax.all_to_all(local_mean, 'replica', split_axis=0, concat_axis=0, tiled=...]
    psum x1 -> x0, blocking collectives: 25.2 us -> none  [layer_pass(): gain_total = lax.psum(gain_local, 'fsdp')]
    reduce_scatter x1 -> x0, waiting for transfers between devices: 25.1 us -> none  [layer_pass(): lax.psum_scatter(lax.dot_general(columns, cotangent, (((0,), (0,)), ((),...]
    all_to_all x1 -> x0, waiting for transfers between devices: 19.6 us -> none  [outer_step(): lax.all_to_all(flat_grad, 'replica', split_axis=0, concat_axis=0, tiled=T...]
    all_to_all x1 -> x0, starting transfers between devices: 19.6 us -> none  [outer_step(): lax.all_to_all(flat_grad, 'replica', split_axis=0, concat_axis=0, tiled=T...]
    dot_general x3 -> x0, matrix products: 11.4 us -> none  [the longest x1 4.06 us: layer_pass(): lax.dot_general(columns, cotangent, (((0,), (0,)), ((), ())), preferred_e...]
    all_to_all x2 -> x0, other arithmetic: 6.64 us -> none  [the longest x1 3.94 us: outer_step(): lax.all_to_all(flat_grad, 'replica', split_axis=0, concat_axis=0, tiled=T...]
  transfers between devices with their start and end apart: 3 -> 0, of which waited for: 2 -> 0; matrix products, arithmetic and copies ran while one was open for 16% -> 0% of each run, Pallas kernels for 0% -> 0%
where the time goes in v2:
time: 81.6 us; the launch traced here: 81.4 us
  Pallas kernels  80.7 us (99%)
    pallas_call x1, Pallas kernels, body(): step(NQ, 0)  78.3 us
    pallas_call x1, Pallas kernels, body(): pl.pallas_call(hand_over, out_shape=results, in_specs=[hbm] * 5, out_spec...  2.4 us

profile of v2, /device:TPU:1, one launch (start us, length us, event | category | flops | bytes accessed | tf_op | source)
XLA Modules:
  0.0 81.4 jit_solution(12763117107463776948)
XLA Ops:
  0.6 78.3 %step_32.1 = (bf16[4,512,128]{2,1,0:T(8,128)(2,1)}, bf16[4,512,128]{2,1,0:T(8,128)(2,1)}, bf16[1,128,512]{2,1,0:T(8,128)(2,1)}, bf16[1,512,512]{2,1,0:T(8,128)(2,1)}, f32[1,4096]{1,0:T(1,128)}) custom-call(s32[64]{0:T(128)} %refs_0_.1, bf16[1,512,512]{2,1,0:T(8,128)(2,1)} %refs_1_.1, bf16[1,512,512]{2,1,0:T(8,128)(2,1)} %refs_2_.1, ...), custom_call_target="tpu_custom_call" | custom-call | tf_op jit(solution)/shard_map/step_32/pallas_call | solution.py:521
  79.0 2.4 %hand_over.1 = (bf16[1,512,512]{2,1,0:T(8,128)(2,1)}, bf16[1,512,512]{2,1,0:T(8,128)(2,1)}, bf16[1,128,512]{2,1,0:T(8,128)(2,1)}, bf16[1,512,512]{2,1,0:T(8,128)(2,1)}, f32[1,4096]{1,0:T(1,128)}) custom-call(bf16[4,512,128]{2,1,0:T(8,128)(2,1)} %get-tuple-element.10.fresh_p, bf16[4,512,128]{2,1,0:T(8,128)(2,1)} %get-tuple-element.11.moment_p, ...), custom_call_target="tpu_custom_call" | custom-call | tf_op jit(solution)/shard_map/hand_over/pallas_call | solution.py:524

commit v3 on v2

--- a/solution.py
+++ b/solution.py
@@ -15,6 +15,7 @@
 NX, NY = 4, 8
 NQ = NX * NY
 REPS = 2 * NQ
+FEW = 22
 NP = 4
 NF = 2 * NP
 TOK = 128
@@ -33,7 +34,7 @@
     cap,
     partner_h, grad_h, mom_h, par_h, act_h, gain_h, w_h, cot_h,
     fresh_h, moment_h, keys_h, wgrad_h, ggrad_h,
-    partner, gain_v, grad_v, mom_v, par_v, act_v, w_v, cot_v,
+    table, table_v, partner_v, gain_v, grad_v, mom_v, par_v, act_v, w_v, cot_v,
     met, packed, beyond, back, mirror, fresh_v, moment_v,
     acts, cots, x_in, x_out, near_in, near_out, far_out, far_in, own_part,
     wide_w, gcol, keys_v, wgrad_v, ggrad_v, rms_v,
@@ -79,7 +80,7 @@
                 (w_h.at[0], w_v),
                 (grad_h.at[0], grad_v),
                 (act_h.at[0, :, block_of(f)], acts.at[f]),
-                (partner_h, partner),
+                (partner_h, partner_v),
                 (mom_h.at[0], mom_v),
                 (par_h.at[0], par_v),
             )
@@ -105,7 +106,7 @@
         return remote(cots.at[b], cots.at[b], cx_send.at[0], c_recv.at[b], (r, f))
 
     def z_copy(s):
-        return remote(met[s], beyond[s], z_send.at[s], z_recv.at[s], (q * 2 + 1 - half, f))
+        return remote(packed[s], beyond[s], z_send.at[s], z_recv.at[s], (q * 2 + 1 - half, f))
 
     def all_but_one(ref, ss, rs):
         return remote(ref.at[pl.ds(0, NQ - 1)], ref.at[pl.ds(0, NQ - 1)], ss, rs, (r, f))
@@ -147,7 +148,7 @@
         inv_rms = lax.rsqrt(jnp.sum(total, axis=-1, keepdims=True) * (1.0 / D) + NORM_EPS)
         rms_v[...] = jnp.broadcast_to(inv_rms, (TOK, 128))
         loads[1].wait()
-        cots[f] = (cot_v[...].astype(f32) * inv_rms).astype(bf16)
+        cot_v[...] = (cot_v[...].astype(f32) * inv_rms).astype(bf16)
         loads[2].wait()
         gcol[...] = jnp.transpose(jnp.broadcast_to(gain_v[:, block_of(f)], (128, BLK)))
         loads[3].wait()
@@ -168,26 +169,48 @@
             lax.fori_loop(1, NQ, send, 0)
             met[s][q] = grad_v[rows_of(q), pl.ds(s * CW, CW)]
 
-    def crossing(i, side):
-        return lax.rem(partner[i * 2 + side] + side, 2)
-
     def tables():
         loads[6].wait()
+        i32 = jnp.int32
+        table_v[...] = jnp.zeros((8, 128), i32)
+        down = lax.broadcasted_iota(i32, (REPS, REPS), 0)
+        along = lax.broadcasted_iota(i32, (REPS, REPS), 1)
+        other = jnp.broadcast_to(partner_v[...], (REPS, REPS))
+        crosses = (other + along) & 1
+        own = jnp.where(down == along, crosses, 0)
+        crosses_down = jnp.broadcast_to(jnp.sum(own, axis=1, keepdims=True), (REPS, REPS))
+        before = jnp.where((down < other) & (((down + other) & 1) == 0), crosses_down, 0)
+        rank_other = jnp.sum(before, axis=0, keepdims=True)
+        row = partner_v[...]
+        row_crosses = (row + along[0:1, :]) & 1
+        table_v[0:1, 0:REPS] = jnp.where(row_crosses == 1, NQ + rank_other, row >> 1)
+        ahead = jnp.where((along < down) & (((along + down) & 1) == 0), crosses, 0)
+        rank = jnp.broadcast_to(jnp.sum(ahead, axis=1, keepdims=True), (REPS, REPS))
+        side, place = along // NQ, along % NQ
+        hit = (crosses_down == 1) & ((down & 1) == side) & (rank == place)
+        table_v[1:2, 0:REPS] = jnp.sum(jnp.where(hit, down >> 1, 0), axis=0, keepdims=True)
+        copy = pltpu.make_async_copy(table_v, table, load_sem.at[9])
+        copy.start()
+        copy.wait()
 
     def leg_z(s):
         all_but_one(met[s], one_send.at[s], one_recv.at[s]).wait_recv()
 
+        def pack(j, carry):
+            packed[s][j] = met[s][table[1, half * NQ + j]]
+            return carry
+
+        lax.fori_loop(0, cap, pack, 0)
         z_copy(s).start()
 
     def leg_two(s):
         z_copy(s).wait_recv()
 
         def mirror_of(to):
-            other = partner[to * 2 + half]
-            i = lax.div(other, 2)
-            here = met[s][i]
-            there = beyond[s][i]
-            return jnp.where(lax.rem(other + half, 2) == 1, there, here)
+            i = table[0, to * 2 + half]
+            here = met[s][jnp.minimum(i, NQ - 1)]
+            there = beyond[s][jnp.clip(i - NQ, 0, cap - 1)]
+            return jnp.where(i >= NQ, there, here)
 
         def send(k, carry):
             to = peer(k)
@@ -216,6 +239,8 @@
         step_out[2 * s + 1].start()
 
     def cots_begin():
+        cots[f] = cot_v[...]
+
         @pl.when(p < NP - 1)
         def _():
             cot_up(p).start()
@@ -347,10 +372,10 @@
     scope = jax.named_scope
     with scope("load"):
         load_and_greet()
+    with scope("norm"):
+        norm()
     with scope("greet"):
         pl.semaphore_wait(barrier, NQ - 1 + 1 + NF - 1)
-    with scope("norm"):
-        norm()
     with scope("send_acts"):
         cots_begin()
         act_copy(p * 2 + 1 - c).start()
@@ -430,7 +455,7 @@
         drain()
 
 def wrapped(cap, *refs):
-    n = 13 + 8
+    n = 13 + 10
     head, rest = refs[:n], refs[n:]
     parts = [rest[i * CUTS : (i + 1) * CUTS] for i in range(7)]
     body_kernel(cap, *head, *parts, *rest[7 * CUTS :])
@@ -481,7 +506,7 @@
 
     def step(cap, collective_id):
         scratch = (
-            [pltpu.SMEM((REPS,), jnp.int32), vmem((1, D), f32)]
+            [pltpu.SMEM((8, 128), jnp.int32), vmem((8, 128), jnp.int32), vmem((1, REPS), jnp.int32), vmem((1, D), f32)]
             + [vmem((BLK, KC), bf16)] * 3
             + [vmem((TOK, D), bf16), vmem((BLK, KC), bf16), vmem((TOK, KC), bf16)]
             + [vmem((NQ, ROWS, CW), bf16)] * CUTS
@@ -500,7 +525,7 @@
                 vmem((1, D), f32),
                 vmem((TOK, 128), f32),
             ]
-            + [dma((9,)), dma((3 + 2 * CUTS,))]
+            + [dma((10,)), dma((3 + 2 * CUTS,))]
             + [dma((CUTS,))] * 6
             + [dma, dma((NF,)), dma((NP,)), dma((NP,)), dma((NP,)), dma((NF,))]
             + [dma((NP,))] * 5
@@ -518,8 +543,11 @@
             name=f"step_{cap}",
         )
 
-    done = step(NQ, 0)(
-        partner, pseudo_grad, momentum, outer_params, activations, norm_gain, key_weight, key_cotangent
+    crossing = jnp.sum(partner.reshape(NQ, 2)[:, 0] % 2)
+    done = lax.cond(
+        crossing <= FEW, step(FEW, 0), step(NQ, 1),
+        partner.reshape(1, REPS), pseudo_grad, momentum, outer_params, activations, norm_gain, key_weight,
+        key_cotangent,
     )
     return pl.pallas_call(
         hand_over,

time: 81.6 us -> 76.2 us (0.934)
  Pallas kernels: 80.7 us -> 72.3 us
  local copies, waits for them, and re-layouts: 0 us -> 0.86 us
    pallas_call x1, Pallas kernels: 78.3 us -> 70.7 us  [body(): lax.cond(crossing <= FEW, step(FEW, 0), step(NQ, 1), partner.reshape(1, R...]
    pallas_call x1, Pallas kernels: 2.4 us -> 1.57 us  [body(): pl.pallas_call(hand_over, out_shape=results, in_specs=[hbm] * 5, out_spec...]
where the time goes in v3:
time: 76.2 us; the launch traced here: 75.1 us
  Pallas kernels  72.3 us (95%)
  between operations  1.32 us (2%)
  local copies, waits for them, and re-layouts  0.86 us (1%)
    pallas_call x1, Pallas kernels, body(): lax.cond(crossing <= FEW, step(FEW, 0), step(NQ, 1), partner.reshape(1, R...  70.7 us
    pallas_call x1, Pallas kernels, body(): pl.pallas_call(hand_over, out_shape=results, in_specs=[hbm] * 5, out_spec...  1.57 us

profile of v3, /device:TPU:1, one launch (start us, length us, event | category | flops | bytes accessed | tf_op | source)
XLA Modules:
  0.0 75.1 jit_solution(10176902991843991881)
XLA Ops:
  0.6 0.0 copy-start.1
  0.6 0.6 copy-done.1
  1.3 0.0 copy-start
  1.3 0.1 reshape.16
  1.4 0.1 slice_reduce_fusion
  1.5 0.6 fusion
  2.8 0.0 copy-done
  2.8 70.7 %conditional.1 = ((bf16[4,512,128]{2,1,0:T(8,128)(2,1)S(1)}, bf16[4,512,128]{2,1,0:T(8,128)(2,1)S(1)}, bf16[1,128,512]{2,1,0:T(8,128)(2,1)S(1)}, bf16[1,512,512]{2,1,0:T(8,128)(2,1)S(1)}, f32[1,4096]{1,0:T(1,128)S(1)})) conditional(s32[]{:T(128)} %convert_element_type.3, (s32[1,64]{1,0:T(1,128)S(1)}, bf16[1,512,512]{2,1,0:T(8,128)(2,1)}, ...), branch_computations={%region_1.2_spmd, %region_2.3_spmd} | conditional | bytes 8 | solution.py:547
  2.8 70.7 %step_22.1 = (bf16[4,512,128]{2,1,0:T(8,128)(2,1)S(1)}, bf16[4,512,128]{2,1,0:T(8,128)(2,1)S(1)}, bf16[1,128,512]{2,1,0:T(8,128)(2,1)S(1)}, bf16[1,512,512]{2,1,0:T(8,128)(2,1)S(1)}, f32[1,4096]{1,0:T(1,128)S(1)}) custom-call(s32[1,64]{1,0:T(1,128)S(1)} %get-tuple-element.40.refs_0_, bf16[1,512,512]{2,1,0:T(8,128)(2,1)} %get-tuple-element.41.refs_1_, ...), custom_call_target="tpu_custom_call" | custom-call | tf_op jit(solution)/shard_map/cond/branch_1_fun/step_22/pallas_call | solution.py:547
  73.6 1.6 %hand_over.1 = (bf16[1,512,512]{2,1,0:T(8,128)(2,1)}, bf16[1,512,512]{2,1,0:T(8,128)(2,1)}, bf16[1,128,512]{2,1,0:T(8,128)(2,1)}, bf16[1,512,512]{2,1,0:T(8,128)(2,1)}, f32[1,4096]{1,0:T(1,128)}) custom-call(bf16[4,512,128]{2,1,0:T(8,128)(2,1)S(1)} %get-tuple-element.58.fresh_p, bf16[4,512,128]{2,1,0:T(8,128)(2,1)S(1)} %get-tuple-element.59.moment_p, ...), custom_call_target="tpu_custom_call" | custom-call | tf_op jit(solution)/shard_map/hand_over/pallas_call | solution.py:552
Async XLA Ops:
  0.6 0.7 copy-start.1
  1.3 1.5 %copy-start = (f32[1,4096]{1,0:T(1,128)S(1)}, f32[1,4096]{1,0:T(1,128)}, u32[]{:S(2)}) copy-start(f32[1,4096]{1,0:T(1,128)} %param.15) | copy-start | bytes 49156

commit v4 on v3

--- a/solution.py
+++ b/solution.py
@@ -154,6 +154,11 @@
         loads[3].wait()
         wide_w[...] = (w_v[...].astype(f32) * gcol[:, 0:1]).astype(bf16)
         loads[4].wait()
+
+    def acts_to(chip, core, condition):
+        @pl.when(condition)
+        def _():
+            act_copy(chip * 2 + core).start()
 
     def leg_one():
         for s in range(CUTS):
@@ -255,7 +260,7 @@
         @pl.when(p >= k)
         def _():
             b = p - k
-            cot_up(b).wait_recv()
+            cot_arrival(b * 2 + c).wait_recv()
             cot_across(b).start()
 
             @pl.when(p < NP - 1)
@@ -265,7 +270,7 @@
         @pl.when(p < NP - k)
         def _():
             b = p + k
-            cot_down(b).wait_recv()
+            cot_arrival(b * 2 + c).wait_recv()
             cot_across(b).start()
 
             @pl.when(p > 0)
@@ -379,15 +384,22 @@
     with scope("send_acts"):
         cots_begin()
         act_copy(p * 2 + 1 - c).start()
-        for chip in (*far_chips, near_chip):
-            for core in (c, 1 - c):
-                act_copy(chip * 2 + core).start()
+        acts_to(NP - 1, c, p < NP - 1)
+        acts_to(0, c, p > 0)
+        acts_to(NP - 1 - p, 1 - c, edge)
+        for chip in (lax.rem(p + 2, NP), lax.rem(p + 1 + 2 * (p // 3), NP)):
+            for e in (c, 1 - c):
+                acts_to(chip, e, edge)
     with scope("leg_one"):
         leg_one()
     with scope("tables"):
         tables()
     with scope("cots_1"):
         cots_onward(1)
+        for chip in (NP - 1, 0):
+            acts_to(chip, 1 - c, inner)
+        for e in (c, 1 - c):
+            acts_to(NP - 1 - p, e, inner)
     with scope("leg_z_0"):
         leg_z(0)
     with scope("leg_z_1"):
@@ -396,6 +408,8 @@
         leg_z(2)
     with scope("leg_z_3"):
         leg_z(3)
+    with scope("cots_2"):
+        cots_onward(2)
     with scope("wait_loads"):
         loads[7].wait()
         loads[8].wait()
@@ -411,26 +425,24 @@
         @pl.when(edge)
         def _():
             sum_near(far_chips[0])
+    with scope("leg_two_2"):
+        leg_two(2)
     with scope("partial_keys_far_2"):
         partial_keys(far_chips[1], False)
     with scope("sum_edge_2"):
         @pl.when(edge)
         def _():
             sum_near(far_chips[1])
-    with scope("cots_2"):
-        cots_onward(2)
     with scope("sum_inner_1"):
         @pl.when(inner)
         def _():
             sum_far(far_chips[0])
+    with scope("partial_keys_near"):
+        partial_keys(near_chip, False)
     with scope("sum_inner_2"):
         @pl.when(inner)
         def _():
             sum_far(far_chips[1])
-    with scope("leg_two_2"):
-        leg_two(2)
-    with scope("partial_keys_near"):
-        partial_keys(near_chip, False)
     with scope("sum_near"):
         sum_near(near_chip)
     with scope("leg_two_3"):
@@ -445,14 +457,15 @@
         outer_step(1)
     with scope("outer_step_2"):
         outer_step(2)
+    with scope("outer_step_3"):
+        outer_step(3)
     with scope("finish_keys"):
         finish_keys()
-    with scope("outer_step_3"):
-        outer_step(3)
     with scope("finish_gain"):
         finish_gain()
     with scope("drain"):
         drain()
+
 
 def wrapped(cap, *refs):
     n = 13 + 10

time: 76.2 us -> 74.8 us (0.982); the launches traced: 75.1 us -> 74.6 us
  no operation moved by 1% of the time
where the time goes in v4:
time: 74.8 us; the launch traced here: 74.6 us
  Pallas kernels  71.8 us (96%)
  between operations  1.32 us (2%)
  local copies, waits for them, and re-layouts  0.86 us (1%)
    pallas_call x1, Pallas kernels, body(): lax.cond(crossing <= FEW, step(FEW, 0), step(NQ, 1), partner.reshape(1, R...  70.2 us
    pallas_call x1, Pallas kernels, body(): pl.pallas_call(hand_over, out_shape=results, in_specs=[hbm] * 5, out_spec...  1.57 us

profile of v4, /device:TPU:1, one launch (start us, length us, event | category | flops | bytes accessed | tf_op | source)
XLA Modules:
  0.0 74.6 jit_solution(9763903443030449957)
XLA Ops:
  0.6 0.0 copy-start.1
  0.6 0.6 copy-done.1
  1.3 0.0 copy-start
  1.3 0.1 reshape.16
  1.4 0.1 slice_reduce_fusion
  1.5 0.6 fusion
  2.8 0.0 copy-done
  2.8 70.2 %conditional.1 = ((bf16[4,512,128]{2,1,0:T(8,128)(2,1)S(1)}, bf16[4,512,128]{2,1,0:T(8,128)(2,1)S(1)}, bf16[1,128,512]{2,1,0:T(8,128)(2,1)S(1)}, bf16[1,512,512]{2,1,0:T(8,128)(2,1)S(1)}, f32[1,4096]{1,0:T(1,128)S(1)})) conditional(s32[]{:T(128)} %convert_element_type.3, (s32[1,64]{1,0:T(1,128)S(1)}, bf16[1,512,512]{2,1,0:T(8,128)(2,1)}, ...), branch_computations={%region_1.2_spmd, %region_2.3_spmd} | conditional | bytes 8 | solution.py:560
  2.8 70.2 %step_22.1 = (bf16[4,512,128]{2,1,0:T(8,128)(2,1)S(1)}, bf16[4,512,128]{2,1,0:T(8,128)(2,1)S(1)}, bf16[1,128,512]{2,1,0:T(8,128)(2,1)S(1)}, bf16[1,512,512]{2,1,0:T(8,128)(2,1)S(1)}, f32[1,4096]{1,0:T(1,128)S(1)}) custom-call(s32[1,64]{1,0:T(1,128)S(1)} %get-tuple-element.40.refs_0_, bf16[1,512,512]{2,1,0:T(8,128)(2,1)} %get-tuple-element.41.refs_1_, ...), custom_call_target="tpu_custom_call" | custom-call | tf_op jit(solution)/shard_map/cond/branch_1_fun/step_22/pallas_call | solution.py:560
  73.1 1.6 %hand_over.1 = (bf16[1,512,512]{2,1,0:T(8,128)(2,1)}, bf16[1,512,512]{2,1,0:T(8,128)(2,1)}, bf16[1,128,512]{2,1,0:T(8,128)(2,1)}, bf16[1,512,512]{2,1,0:T(8,128)(2,1)}, f32[1,4096]{1,0:T(1,128)}) custom-call(bf16[4,512,128]{2,1,0:T(8,128)(2,1)S(1)} %get-tuple-element.58.fresh_p, bf16[4,512,128]{2,1,0:T(8,128)(2,1)S(1)} %get-tuple-element.59.moment_p, ...), custom_call_target="tpu_custom_call" | custom-call | tf_op jit(solution)/shard_map/hand_over/pallas_call | solution.py:565
Async XLA Ops:
  0.6 0.7 copy-start.1
  1.3 1.5 %copy-start = (f32[1,4096]{1,0:T(1,128)S(1)}, f32[1,4096]{1,0:T(1,128)}, u32[]{:S(2)}) copy-start(f32[1,4096]{1,0:T(1,128)} %param.15) | copy-start | bytes 49156
